TPU v7x, 256 devices: a whole 4x4x8 slice. The times are simulated.
256 devices in a mesh: chan: 8 (over z), rad: 32 (over y, x, core).
Axes of the slice: x: 4, y: 4, z: 8, core: 2. Of those that a mesh axis runs over, the one named last changes fastest.
Arguments:
- wavefunc: float32 [2, 2048, 16384], P(None, 'chan', 'rad'), may hold values from -6 to 6
- orbitals: float32 [9, 16384], P(None, 'rad'), may hold values from -6 to 6
- channel_orbital: int32 [2048], P('chan'), may hold values from 0 to 8
- channel_l: int32 [2048], P('chan'), may hold values from 0 to 400
- row_order: int32 [144], replicated, may hold values from 0 to 15
- density_coupling: float32 [144, 2048], P(None, 'chan'), may hold values from -0.125 to 0.125
- field_coupling: float32 [2048, 144], P('chan'), may hold values from -6 to 6
Outputs:
- advanced: float32 [2, 2048, 16384], P(None, 'chan', 'rad')
All inputs are finite; a program needn't handle non-finite values.
Results may differ from a plain program's by a relative error of at most 0.00021.
Values sent between devices are 32-bit elements; how exact they have to be, the bound alone decides.
A program may use at most 64 MiB of HBM per device.

v0:
```python
import functools

import jax
import jax.numpy as jnp
from jax import lax
from jax.experimental import pallas as pl
from jax.experimental.pallas import tpu as pltpu
from jax.sharding import PartitionSpec as P

SWEEPS = 4
MESH = pl.DeviceIdType.MESH
F32 = jnp.float32
BF16 = jnp.bfloat16
LANES = 128
SPAN = 400.0 / 408.0

RS_PLAN = ((-4, -2), (-3, -1), (3, 1), (-1, -1), (1, 1), (-2, -2), (2, 2))
AG_PLAN = ((0, 2), (0, -2), (0, 1), (0, -1), (-2, 2), (-2, 1), (2, -1))
PARTS = ((0, 40), (40, 32))
ROWS_STEP = 32


def split2(x):
    hi = x.astype(BF16)
    return hi, (x - hi.astype(F32)).astype(BF16)


def dot(a, b):
    return jnp.dot(a, b, preferred_element_type=F32)


def as_column(row):
    eight = jnp.broadcast_to(row, (8, row.shape[1]))
    first = lax.broadcasted_iota(jnp.int32, (8, LANES), 0) == 0
    return lax.dot_general(
        eight,
        jnp.where(first, 1.0, 0.0).astype(F32),
        (((0,), (0,)), ((), ())),
        precision=lax.Precision.HIGHEST,
        preferred_element_type=F32,
    )


def kernel(
    sizes,
    wave_hbm,
    orbitals_ref,
    which_ref,
    ell_ref,
    order_ref,
    density_ref,
    coupling_ref,
    out_hbm,
    vbuf,
    rhs,
    orb,
    diag,
    scl,
    field,
    up_t,
    dn_t,
    d_hi,
    d_lo,
    f_hi,
    f_lo,
    rho,
    pot,
    rsbuf,
    own,
    tin01,
    sc_in,
    sc_out,
    ca_src,
    ca_buf,
    cb_src,
    cb_buf,
    cc_src,
    cc_buf,
    io_sem,
    rs_s,
    rs_r,
    ag_s,
    ag_r,
    ca_s,
    ca_r,
    cb_s,
    cb_r,
    cc_s,
    cc_r,
    ha_s,
    ha_r,
):
    nz, nr, ng, chans, width, half = sizes
    ny = nr // ng
    z = lax.axis_index("chan")
    r = lax.axis_index("rad")
    g = lax.rem(r, ng)
    y = lax.div(r, ng)
    total_rows = width * nr
    delta = SPAN / total_rows

    def zdev(offset):
        return (lax.rem(z + offset + nz, nz), r)

    sign = 1 - 2 * lax.rem(r, 2)

    def near(offset):
        return lax.rem(z + sign * offset + nz, nz)

    def gdev(k):
        return (z, y * ng + lax.rem(g + k, ng))

    def ydev(k):
        return (z, lax.rem(y + k, ny) * ng + g)

    load = pltpu.make_async_copy(
        wave_hbm, vbuf.at[0, :, :, pl.ds(LANES, width)], io_sem.at[0]
    )
    load.start()

    zeros_edge = jnp.zeros((chans, LANES), F32)
    for par in range(2):
        for p in range(2):
            vbuf[par, p, :, 0:LANES] = zeros_edge
            vbuf[par, p, :, LANES + width : 2 * LANES + width] = zeros_edge

    barrier = pltpu.get_barrier_semaphore()

    def greet(device):
        pl.semaphore_signal(barrier, inc=1, device_id=device, device_id_type=MESH)

    for k in (1, 2, nz - 2, nz - 1):
        greet(zdev(k))
    for k in range(1, ng):
        greet(gdev(k))
    for k in range(1, ny):
        greet(ydev(k))

    tiles = width // LANES
    i0 = lax.broadcasted_iota(jnp.int32, (LANES, LANES), 0)
    i1 = lax.broadcasted_iota(jnp.int32, (LANES, LANES), 1)
    tri_in = jnp.where(i0 <= i1, 1.0, 0.0).astype(BF16)
    tri_out = jnp.where(i0 > i1, 1.0, 0.0).astype(BF16)
    lane_id = lax.broadcasted_iota(jnp.int32, (half, LANES), 1)

    def spread_orbitals():
        which = as_column(which_ref[...].astype(F32))
        for t in range(tiles):
            lanes = slice(t * LANES, (t + 1) * LANES)
            for c0 in range(0, chans, ROWS_STEP):
                rows = slice(c0, c0 + ROWS_STEP)
                pick = which[rows]
                value = jnp.zeros((ROWS_STEP, LANES), F32)
                for o in range(orbitals_ref.shape[0]):
                    value = jnp.where(pick == float(o), orbitals_ref[o : o + 1, lanes], value)
                orb[rows, lanes] = value
        hi, lo = split2(density_ref[...])
        d_hi[...] = hi
        d_lo[...] = lo

    def radius_of(t):
        lane = lax.broadcasted_iota(jnp.int32, (1, LANES), 1)
        index = (r * width + t * LANES + lane).astype(F32)
        return 8.0 + 400.0 * (index + 0.5) / total_rows

    def power_tables():
        order = as_column(order_ref[...].astype(F32))
        for t in range(tiles):
            scaled = radius_of(t) / 408.0
            up = jnp.exp(order * jnp.log(scaled))
            dn = 1.0 / (up * scaled)
            inv_dn = jnp.broadcast_to((up * scaled)[:, LANES - 1 :], up.shape)
            inv_up = jnp.broadcast_to((dn * scaled)[:, :1], up.shape)
            for mh in range(2):
                rows = slice(mh * half, (mh + 1) * half)
                up_t[t, mh] = up[rows]
                dn_t[t, mh] = dn[rows]
                sc_in[t, mh] = inv_dn[rows]
                sc_out[t, mh] = inv_up[rows]

    def diagonal_tables():
        ell = as_column(ell_ref[...].astype(F32))
        strength = ell * (ell + 1.0)
        for t in range(tiles):
            radius = radius_of(t)
            inv = 1.0 / (4.0 * radius * radius)
            lanes = slice(t * LANES, (t + 1) * LANES)
            for c0 in range(0, chans, ROWS_STEP):
                rows = slice(c0, c0 + ROWS_STEP)
                dg = 0.5 + strength[rows] * inv
                diag[rows, lanes] = dg
                scl[rows, lanes] = 1.0 / (1.0 + dg * dg)
        turned = jnp.concatenate(
            [coupling_ref[...], jnp.zeros((chans - 2 * half, chans), F32)], axis=0
        )
        hi, lo = split2(jnp.transpose(turned)[:, : 2 * half])
        f_hi[...] = hi
        f_lo[...] = lo
        rhs[...] = jnp.zeros_like(rhs)

    def rs_copy(pc, part, i):
        chunk, target = RS_PLAN[i]
        rows = pl.ds(*PARTS[part])
        return pltpu.make_async_remote_copy(
            src_ref=rho.at[pc, near(chunk), rows],
            dst_ref=rsbuf.at[pc, i, rows],
            send_sem=rs_s.at[pc, part, i],
            recv_sem=rs_r.at[pc, part, i],
            device_id=(near(target), r),
            device_id_type=MESH,
        )

    def ag_copy(pc, part, i):
        chunk, target = AG_PLAN[i]
        place = pot.at[pc, near(chunk), pl.ds(*PARTS[part])]
        return pltpu.make_async_remote_copy(
            src_ref=place,
            dst_ref=place,
            send_sem=ag_s.at[pc, part, i],
            recv_sem=ag_r.at[pc, part, i],
            device_id=(near(target), r),
            device_id_type=MESH,
        )

    def small_copy(src, buf, send, recv, par, k, device):
        return pltpu.make_async_remote_copy(
            src_ref=src,
            dst_ref=buf.at[par, k - 1],
            send_sem=send.at[k - 1],
            recv_sem=recv.at[par, k - 1],
            device_id=device,
            device_id_type=MESH,
        )

    def ca_copy(par, k):
        return small_copy(ca_src, ca_buf, ca_s, ca_r, par, k, gdev(k))

    def cb_copy(par, k):
        return small_copy(cb_src, cb_buf, cb_s, cb_r, par, k, ydev(k))

    def cc_copy(par, k):
        return small_copy(cc_src, cc_buf, cc_s, cc_r, par, k, zdev(k))

    def halo_copy(par, side):
        here, there = (width, 0) if side == 0 else (LANES, LANES + width)
        to = r + 1 if side == 0 else r - 1
        to = lax.rem(to + nr, nr)
        return pltpu.make_async_remote_copy(
            src_ref=vbuf.at[par, :, :, pl.ds(here, LANES)],
            dst_ref=vbuf.at[par, :, :, pl.ds(there, LANES)],
            send_sem=ha_s.at[side],
            recv_sem=ha_r.at[par, side],
            device_id=(z, to),
            device_id_type=MESH,
        )

    def densities(par, pc):
        base = pc * 2 * LANES
        for p in range(2):
            weighted = (
                vbuf[par, p, :, pl.ds(LANES + base, 2 * LANES)] * orb[:, base : base + 2 * LANES]
            )
            hi, lo = split2(weighted)
            part = dot(d_hi[...], hi) + (dot(d_hi[...], lo) + dot(d_lo[...], hi))
            for mh in range(2):
                for h in range(2):
                    rho[pc, 4 * p + 2 * mh + h] = part[
                        mh * half : (mh + 1) * half, h * LANES : (h + 1) * LANES
                    ]

    def send_far(pc):
        for part in range(len(PARTS)):
            for i in (0, 1, 2):
                rs_copy(pc, part, i).start()

    def send_direct():
        for pc in range(2):
            for part in range(len(PARTS)):
                for i in (3, 4):
                    rs_copy(pc, part, i).start()

    def totals(par):
        acc = jnp.zeros((half, LANES), F32)
        for p in range(2):
            for mh in range(2):
                blocks = [rho[t // 2, 4 * p + 2 * mh + t % 2] * delta for t in range(tiles)]
                ups = [blocks[t] * up_t[t, mh] for t in range(tiles)]
                dns = [blocks[t] * dn_t[t, mh] for t in range(tiles)]
                near_out = dns[0] + dns[1]
                far_out = dns[2] + dns[3]
                sums = ((ups[0] + ups[1]) + (ups[2] + ups[3]), near_out + far_out, far_out)
                for kind in range(3):
                    s = jnp.sum(sums[kind], axis=1, keepdims=True)
                    acc = jnp.where(lane_id == kind * 4 + p * 2 + mh, s, acc)
        full = jnp.concatenate([acc, jnp.zeros((LANES - half, LANES), F32)], axis=0)
        own[...] = jnp.transpose(full)[0:16]
        ca_src[0] = own[0:4]
        ca_src[1] = own[4:8]
        for k in range(1, ng):
            ca_copy(par, k).start()

    def communicate(par):
        for pc in range(2):
            for part in range(len(PARTS)):
                rows = pl.ds(*PARTS[part])
                rs_copy(pc, part, 0).wait_recv()
                rs_copy(pc, part, 1).wait_recv()
                at = near(-2)
                rho[pc, at, rows] = rho[pc, at, rows] + rsbuf[pc, 0, rows] + rsbuf[pc, 1, rows]
                rs_copy(pc, part, 5).start()
                rs_copy(pc, part, 2).wait_recv()
                at = near(2)
                rho[pc, at, rows] = rho[pc, at, rows] + rsbuf[pc, 2, rows]
                rs_copy(pc, part, 6).start()
        below = jnp.zeros((4, LANES), F32)
        above = jnp.zeros((4, LANES), F32)
        whole_in = ca_src[0]
        whole_out = ca_src[1]
        for k in range(1, ng):
            ca_copy(par, k).wait_recv()
            peer = lax.rem(g - k + ng, ng)
            got_in = ca_buf[par, k - 1, 0]
            got_out = ca_buf[par, k - 1, 1]
            below = below + got_in * jnp.where(peer < g, 1.0, 0.0).astype(F32)
            above = above + got_out * jnp.where(peer > g, 1.0, 0.0).astype(F32)
            whole_in = whole_in + got_in
            whole_out = whole_out + got_out
        cb_src[0] = whole_in
        cb_src[1] = whole_out
        for k in range(1, ny):
            cb_copy(par, k).start()

        @pl.when(r < nr - 1)
        def _():
            halo_copy(par, 0).start()

        @pl.when(r > 0)
        def _():
            halo_copy(par, 1).start()

        quarter = lax.rem(lax.div(z, 2), 2)
        for pc in range(2):
            tile = 2 * pc + lax.rem(z, 2)
            for part in range(len(PARTS)):
                size = PARTS[part][1]
                rows = pl.ds(*PARTS[part])
                for i in (3, 4, 5, 6):
                    rs_copy(pc, part, i).wait_recv()
                acc = (rho[pc, z, rows] + rsbuf[pc, 3, rows]) + (
                    rsbuf[pc, 4, rows] + rsbuf[pc, 5, rows]
                )
                acc = (acc + rsbuf[pc, 6, rows]) * delta
                up = up_t[tile, quarter, rows]
                dn = dn_t[tile, quarter, rows]

                def local(x, tri):
                    hi = x.astype(BF16).astype(F32)
                    both = jnp.concatenate([hi, x - hi], axis=0).astype(BF16)
                    s = dot(both, tri)
                    return s[:size] + s[size:]

                pot[pc, z, rows] = dn * local(acc * up, tri_in) + up * local(acc * dn, tri_out)
                for i in range(4):
                    ag_copy(pc, part, i).start()
        for k in range(1, ny):
            cb_copy(par, k).wait_recv()
            peer = lax.rem(y - k + ny, ny)
            below = below + cb_buf[par, k - 1, 0] * jnp.where(peer < y, 1.0, 0.0).astype(F32)
            above = above + cb_buf[par, k - 1, 1] * jnp.where(peer > y, 1.0, 0.0).astype(F32)
        cc_src[0] = below
        cc_src[1] = above + own[8:12]
        cc_src[2] = above
        for k in range(1, nz):
            cc_copy(par, k).start()
        for pc in range(2):
            for part in range(len(PARTS)):
                ag_copy(pc, part, 0).wait_recv()
                ag_copy(pc, part, 4).start()
                ag_copy(pc, part, 5).start()
                ag_copy(pc, part, 1).wait_recv()
                ag_copy(pc, part, 6).start()
        carry = [cc_src[kind] for kind in range(3)]
        for k in range(1, nz):
            cc_copy(par, k).wait_recv()
            carry = [carry[kind] + cc_buf[par, k - 1, kind] for kind in range(3)]
        for pc in range(2):
            for part in range(len(PARTS)):
                for i in range(7):
                    rs_copy(pc, part, i).wait_send()
        for k in range(1, ng):
            ca_copy(par, k).wait_send()
        for k in range(1, ny):
            cb_copy(par, k).wait_send()
        for k in range(1, nz):
            cc_copy(par, k).wait_send()

        @pl.when(r < nr - 1)
        def _():
            halo_copy(par, 0).wait_send()
            halo_copy(par, 1).wait_recv()

        @pl.when(r > 0)
        def _():
            halo_copy(par, 1).wait_send()
            halo_copy(par, 0).wait_recv()

        for kind in range(3):
            own[4 * kind : 4 * kind + 4] = carry[kind]
        pad = jnp.zeros((LANES - 16, LANES), F32)
        return jnp.transpose(jnp.concatenate([own[...], pad], axis=0))[:half]

    def advance(n, par, pc, carry):
        base = pc * 2 * LANES
        for part in range(len(PARTS)):
            for i in (2, 3, 4, 5, 6):
                ag_copy(pc, part, i).wait_recv()
            for i in range(7):
                ag_copy(pc, part, i).wait_send()
        for p in range(2):
            cols = [[], []]
            for mh in range(2):
                k = 2 * p + mh
                t = 2 * pc
                first_pot = pot[pc, 4 * p + 2 * mh]
                second_pot = pot[pc, 4 * p + 2 * mh + 1]
                wide = (half, LANES)
                below = jnp.broadcast_to(carry[:, k : k + 1], wide)
                at = 4 * (pc + 1) + k
                above = jnp.broadcast_to(carry[:, at : at + 1], wide)
                in_first = jnp.broadcast_to(first_pot[:, LANES - 1 :], wide) * sc_in[t, mh]
                out_second = jnp.broadcast_to(second_pot[:, :1], wide) * sc_out[t + 1, mh]
                if pc == 0:
                    in_second = jnp.broadcast_to(second_pot[:, LANES - 1 :], wide)
                    tin01[k] = in_first + in_second * sc_in[t + 1, mh]
                else:
                    below = below + tin01[k]
                cols[0].append(
                    first_pot + dn_t[t, mh] * below + up_t[t, mh] * (above + out_second)
                )
                cols[1].append(
                    second_pot + dn_t[t + 1, mh] * (below + in_first) + up_t[t + 1, mh] * above
                )
            cols = [jnp.concatenate(parts, axis=0) for parts in cols]
            hi, lo = split2(jnp.concatenate(cols, axis=1))
            field[p] = dot(f_hi[...], hi) + (dot(f_hi[...], lo) + dot(f_lo[...], hi))
        first = n == 0
        for c0 in range(0, chans, ROWS_STEP):
            rows = slice(c0, c0 + ROWS_STEP)
            lanes = slice(base, base + 2 * LANES)
            ob = orb[rows, lanes]
            v, w = [], []
            for p in range(2):
                x = vbuf[par, p, rows, pl.ds(base, 4 * LANES)]
                left = pltpu.roll(x, 1, 1)[:, LANES : 3 * LANES]
                right = pltpu.roll(x, 4 * LANES - 1, 1)[:, LANES : 3 * LANES]
                v.append(x[:, LANES : 3 * LANES])
                w.append(field[p, rows, :] * ob - 0.25 * (left + right))
            dg = diag[rows, lanes]
            r0 = jnp.where(first, v[0] + (w[1] + dg * v[1]), rhs[0, rows, lanes])
            r1 = jnp.where(first, v[1] - (w[0] + dg * v[0]), rhs[1, rows, lanes])
            rhs[0, rows, lanes] = r0
            rhs[1, rows, lanes] = r1
            n0 = r0 + w[1]
            n1 = r1 - w[0]
            sc = scl[rows, lanes]
            vbuf[1 - par, 0, rows, pl.ds(LANES + base, 2 * LANES)] = (n0 + dg * n1) * sc
            vbuf[1 - par, 1, rows, pl.ds(LANES + base, 2 * LANES)] = (n1 - dg * n0) * sc

    spread_orbitals()
    load.wait()
    densities(0, 0)
    pl.semaphore_wait(barrier, 4 + (ng - 1) + (ny - 1))
    send_far(0)
    densities(0, 1)
    send_far(1)
    send_direct()
    power_tables()
    totals(0)
    diagonal_tables()

    def store(pc):
        at = pc * 2 * LANES
        return pltpu.make_async_copy(
            vbuf.at[SWEEPS % 2, :, :, pl.ds(LANES + at, 2 * LANES)],
            out_hbm.at[:, :, pl.ds(at, 2 * LANES)],
            io_sem.at[pc],
        )

    def sweep(n, c):
        par = lax.rem(n, 2)
        carry = communicate(par)
        for pc in range(2):
            advance(n, par, pc, carry)

            @pl.when(n < SWEEPS - 1)
            def _():
                densities(1 - par, pc)
                send_far(pc)

            @pl.when(n == SWEEPS - 1)
            def _():
                store(pc).start()

        @pl.when(n < SWEEPS - 1)
        def _():
            send_direct()
            totals(1 - par)

        return c

    lax.fori_loop(0, SWEEPS, sweep, 0)
    for pc in range(2):
        store(pc).wait()


def body(nz, nr, wavefunc, orbitals, channel_orbital, channel_l, row_order, density, coupling):
    chans, width = wavefunc.shape[1:]
    rows = row_order.shape[0]
    half = rows // 2
    ng = 8 if nr % 8 == 0 else 2
    ny = nr // ng
    vmem = pl.BlockSpec(memory_space=pltpu.VMEM)
    hbm = pl.BlockSpec(memory_space=pl.ANY)
    dma = pltpu.SemaphoreType.DMA
    scratch = [
        pltpu.VMEM((2, 2, chans, width + 2 * LANES), F32),
        pltpu.VMEM((2, chans, width), F32),
        pltpu.VMEM((chans, width), F32),
        pltpu.VMEM((chans, width), F32),
        pltpu.VMEM((chans, width), F32),
        pltpu.VMEM((2, chans, 2 * LANES), F32),
        pltpu.VMEM((4, 2, half, LANES), F32),
        pltpu.VMEM((4, 2, half, LANES), F32),
        pltpu.VMEM((rows, chans), BF16),
        pltpu.VMEM((rows, chans), BF16),
        pltpu.VMEM((chans, rows), BF16),
        pltpu.VMEM((chans, rows), BF16),
        pltpu.VMEM((2, 8, half, LANES), F32),
        pltpu.VMEM((2, 8, half, LANES), F32),
        pltpu.VMEM((2, 7, half, LANES), F32),
        pltpu.VMEM((16, LANES), F32),
        pltpu.VMEM((4, half, LANES), F32),
        pltpu.VMEM((4, 2, half, LANES), F32),
        pltpu.VMEM((4, 2, half, LANES), F32),
        pltpu.VMEM((2, 4, LANES), F32),
        pltpu.VMEM((2, ng - 1, 2, 4, LANES), F32),
        pltpu.VMEM((2, 4, LANES), F32),
        pltpu.VMEM((2, ny - 1, 2, 4, LANES), F32),
        pltpu.VMEM((3, 4, LANES), F32),
        pltpu.VMEM((2, nz - 1, 3, 4, LANES), F32),
        dma((2,)),
        dma((2, len(PARTS), 7)),
        dma((2, len(PARTS), 7)),
        dma((2, len(PARTS), 7)),
        dma((2, len(PARTS), 7)),
        dma((ng - 1,)),
        dma((2, ng - 1)),
        dma((ny - 1,)),
        dma((2, ny - 1)),
        dma((nz - 1,)),
        dma((2, nz - 1)),
        dma((2,)),
        dma((2, 2)),
    ]
    return pl.pallas_call(
        functools.partial(kernel, (nz, nr, ng, chans, width, half)),
        out_shape=jax.ShapeDtypeStruct(wavefunc.shape, F32),
        in_specs=[hbm] + [vmem] * 6,
        out_specs=hbm,
        scratch_shapes=scratch,
        compiler_params=pltpu.CompilerParams(
            collective_id=0, has_side_effects=True, vmem_limit_bytes=48 << 20
        ),
        name="cn_step",
    )(
        wavefunc,
        orbitals,
        channel_orbital.reshape(1, chans),
        channel_l.reshape(1, chans),
        row_order.reshape(1, rows),
        density,
        coupling.T,
    )


def solution(mesh):
    placed = (
        P(None, "chan", "rad"),
        P(None, "rad"),
        P("chan"),
        P("chan"),
        P(),
        P(None, "chan"),
        P("chan", None),
    )
    return jax.shard_map(
        functools.partial(body, mesh.shape["chan"], mesh.shape["rad"]),
        mesh=mesh,
        in_specs=placed,
        out_specs=P(None, "chan", "rad"),
        check_vma=False,
    )
```

profile of v0, /device:TPU:32, one launch (start us, length us, event | category | flops | bytes accessed | tf_op | source)
XLA Modules:
  0.0 95.1 jit_solution(12514136105606328797)
XLA Ops:
  0.0 0.0 copy-start.5
  0.0 0.0 copy-start.6
  0.0 0.0 copy-start.4
  0.0 0.7 copy-done.5
  0.7 0.0 copy-done.6
  0.7 0.0 copy-done.4
  0.7 0.0 copy-start
  0.7 1.2 %copy-done = f32[2,256,512]{2,1,0:T(8,128)S(1)} copy-done((f32[2,256,512]{2,1,0:T(8,128)S(1)}, f32[2,256,512]{2,1,0:T(8,128)}, u32[]{:S(2)}) %copy-start) | copy-done | bytes 1048600
  1.9 0.0 copy-start.1
  1.9 0.9 copy-done.1
  2.8 0.0 copy-start.2
  2.8 0.9 copy-done.2
  3.8 0.0 copy-start.3
  3.8 0.8 copy-done.3
  4.5 89.6 %cn_step.1 = f32[2,256,512]{2,1,0:T(8,128)S(1)} custom-call(f32[2,256,512]{2,1,0:T(8,128)S(1)} %copy-done, f32[9,512]{1,0:T(8,128)S(1)} %copy-done.3, s32[1,256]{1,0:T(1,128)S(1)} %bitcast.5, s32[1,256]{1,0:T(1,128)S(1)} %bitcast.6, s32[1,144]{1,0:T(1,128)S(1)} %bitcast.7, f32[144,256]{1,0:T(8,128)S(1)} %copy-done.1, f32[144,256]{1,0:T(8,128)S(1)} %bitcast.4), custom_call_target="tpu_custom_call" | custom-call | tf_op jit(solution)/shard_map/cn_step/pallas_call | solution.py:565
  94.2 1.0 %copy.9 = f32[2,256,512]{2,1,0:T(8,128)} copy(f32[2,256,512]{2,1,0:T(8,128)S(1)} %cn_step.1) | data formatting | bytes 2097152
Async XLA Ops:
  0.0 0.7 copy-start.5
  0.0 0.7 copy-start.6
  0.0 0.7 copy-start.4
  0.7 1.2 %copy-start = (f32[2,256,512]{2,1,0:T(8,128)S(1)}, f32[2,256,512]{2,1,0:T(8,128)}, u32[]{:S(2)}) copy-start(f32[2,256,512]{2,1,0:T(8,128)} %wave_hbm.1) | copy-start | bytes 3145732
  1.9 0.9 copy-start.1
  2.8 0.9 copy-start.2
  3.8 0.8 copy-start.3
where the time goes:
time: 96.7 us; the launch traced here: 95.1 us
  Pallas kernels  89.6 us (93%)
  local copies, waits for them, and re-layouts  5.48 us (6%)
    pallas_call x1, Pallas kernels, body(): pl.pallas_call(functools.partial(kernel, (nz, nr, ng, chans, width, half)...  89.6 us
    unnamed x15, local copies, waits for them, and re-layouts  5.48 us

commit v1 on v0

--- a/solution.py
+++ b/solution.py
@@ -56,13 +56,16 @@
     orb,
     diag,
     scl,
+    known,
+    alpha,
+    beta,
     field,
+    w_hi,
+    w_lo,
     up_t,
     dn_t,
-    d_hi,
-    d_lo,
-    f_hi,
-    f_lo,
+    d_both,
+    f_both,
     rho,
     pot,
     rsbuf,
@@ -155,8 +158,8 @@
                     value = jnp.where(pick == float(o), orbitals_ref[o : o + 1, lanes], value)
                 orb[rows, lanes] = value
         hi, lo = split2(density_ref[...])
-        d_hi[...] = hi
-        d_lo[...] = lo
+        d_both[: 2 * half] = hi
+        d_both[2 * half :] = lo
 
     def radius_of(t):
         lane = lax.broadcasted_iota(jnp.int32, (1, LANES), 1)
@@ -188,15 +191,18 @@
             for c0 in range(0, chans, ROWS_STEP):
                 rows = slice(c0, c0 + ROWS_STEP)
                 dg = 0.5 + strength[rows] * inv
+                sc = 1.0 / (1.0 + dg * dg)
+                al = sc * orb[rows, lanes]
                 diag[rows, lanes] = dg
-                scl[rows, lanes] = 1.0 / (1.0 + dg * dg)
+                scl[rows, lanes] = sc
+                alpha[rows, lanes] = al
+                beta[rows, lanes] = al * dg
         turned = jnp.concatenate(
             [coupling_ref[...], jnp.zeros((chans - 2 * half, chans), F32)], axis=0
         )
         hi, lo = split2(jnp.transpose(turned)[:, : 2 * half])
-        f_hi[...] = hi
-        f_lo[...] = lo
-        rhs[...] = jnp.zeros_like(rhs)
+        f_both[:chans] = hi
+        f_both[chans:] = lo
 
     def rs_copy(pc, part, i):
         chunk, target = RS_PLAN[i]
@@ -254,30 +260,77 @@
             device_id_type=MESH,
         )
 
-    def densities(par, pc):
-        base = pc * 2 * LANES
+    def weigh(par, pc):
+        lanes = slice(pc * 2 * LANES, (pc + 1) * 2 * LANES)
+        for c0 in range(0, chans, ROWS_STEP):
+            rows = slice(c0, c0 + ROWS_STEP)
+            for p in range(2):
+                v = vbuf[par, p, rows, LANES + lanes.start : LANES + lanes.stop]
+                hi, lo = split2(v * orb[rows, lanes])
+                w_hi[p, rows] = hi
+                w_lo[p, rows] = lo
+
+    def densities(pc):
+        rows = 2 * half
         for p in range(2):
-            weighted = (
-                vbuf[par, p, :, pl.ds(LANES + base, 2 * LANES)] * orb[:, base : base + 2 * LANES]
-            )
-            hi, lo = split2(weighted)
-            part = dot(d_hi[...], hi) + (dot(d_hi[...], lo) + dot(d_lo[...], hi))
+            wide = dot(d_both[...], w_hi[p])
+            part = wide[:rows] + (wide[rows:] + dot(d_both[:rows], w_lo[p]))
             for mh in range(2):
                 for h in range(2):
                     rho[pc, 4 * p + 2 * mh + h] = part[
                         mh * half : (mh + 1) * half, h * LANES : (h + 1) * LANES
                     ]
 
+    def prepare(n, par, pc):
+        base = pc * 2 * LANES
+        lanes = slice(base, base + 2 * LANES)
+
+        def kinetic(rows):
+            v, kin = [], []
+            for p in range(2):
+                x = vbuf[par, p, rows, pl.ds(base, 4 * LANES)]
+                left = pltpu.roll(x, 1, 1)[:, LANES : 3 * LANES]
+                right = pltpu.roll(x, 4 * LANES - 1, 1)[:, LANES : 3 * LANES]
+                v.append(x[:, LANES : 3 * LANES])
+                kin.append(-0.25 * (left + right))
+            return v, kin
+
+        @pl.when(n == 0)
+        def _():
+            for c0 in range(0, chans, ROWS_STEP):
+                rows = slice(c0, c0 + ROWS_STEP)
+                v, kin = kinetic(rows)
+                dg = diag[rows, lanes]
+                rhs[0, rows, lanes] = v[0] + (kin[1] + dg * v[1])
+                rhs[1, rows, lanes] = v[1] - (kin[0] + dg * v[0])
+
+        @pl.when(n == 1)
+        def _():
+            for c0 in range(0, chans, ROWS_STEP):
+                rows = slice(c0, c0 + ROWS_STEP)
+                ob = orb[rows, lanes]
+                rhs[0, rows, lanes] = rhs[0, rows, lanes] + field[pc, 1, rows] * ob
+                rhs[1, rows, lanes] = rhs[1, rows, lanes] - field[pc, 0, rows] * ob
+
+        for c0 in range(0, chans, ROWS_STEP):
+            rows = slice(c0, c0 + ROWS_STEP)
+            v, kin = kinetic(rows)
+            dg = diag[rows, lanes]
+            sc = scl[rows, lanes]
+            q0 = rhs[0, rows, lanes] + kin[1]
+            q1 = rhs[1, rows, lanes] - kin[0]
+            known[0, rows, lanes] = (q0 + dg * q1) * sc
+            known[1, rows, lanes] = (q1 - dg * q0) * sc
+
     def send_far(pc):
         for part in range(len(PARTS)):
             for i in (0, 1, 2):
                 rs_copy(pc, part, i).start()
 
-    def send_direct():
-        for pc in range(2):
-            for part in range(len(PARTS)):
-                for i in (3, 4):
-                    rs_copy(pc, part, i).start()
+    def send_direct(pc):
+        for part in range(len(PARTS)):
+            for i in (3, 4):
+                rs_copy(pc, part, i).start()
 
     def totals(par):
         acc = jnp.zeros((half, LANES), F32)
@@ -299,7 +352,7 @@
         for k in range(1, ng):
             ca_copy(par, k).start()
 
-    def communicate(par):
+    def communicate(n, par):
         for pc in range(2):
             for part in range(len(PARTS)):
                 rows = pl.ds(*PARTS[part])
@@ -312,6 +365,8 @@
                 at = near(2)
                 rho[pc, at, rows] = rho[pc, at, rows] + rsbuf[pc, 2, rows]
                 rs_copy(pc, part, 6).start()
+            if pc == 0:
+                send_direct(1)
         below = jnp.zeros((4, LANES), F32)
         above = jnp.zeros((4, LANES), F32)
         whole_in = ca_src[0]
@@ -360,8 +415,12 @@
                     return s[:size] + s[size:]
 
                 pot[pc, z, rows] = dn * local(acc * up, tri_in) + up * local(acc * dn, tri_out)
-                for i in range(4):
+                for i in (0, 1):
                     ag_copy(pc, part, i).start()
+            if pc == 0:
+                for part in range(len(PARTS)):
+                    for i in (2, 3):
+                        ag_copy(pc, part, i).start()
         for k in range(1, ny):
             cb_copy(par, k).wait_recv()
             peer = lax.rem(y - k + ny, ny)
@@ -372,6 +431,18 @@
         cc_src[2] = above
         for k in range(1, nz):
             cc_copy(par, k).start()
+
+        @pl.when(r < nr - 1)
+        def _():
+            halo_copy(par, 0).wait_send()
+            halo_copy(par, 1).wait_recv()
+
+        @pl.when(r > 0)
+        def _():
+            halo_copy(par, 1).wait_send()
+            halo_copy(par, 0).wait_recv()
+
+        prepare(n, par, 0)
         for pc in range(2):
             for part in range(len(PARTS)):
                 ag_copy(pc, part, 0).wait_recv()
@@ -379,6 +450,11 @@
                 ag_copy(pc, part, 5).start()
                 ag_copy(pc, part, 1).wait_recv()
                 ag_copy(pc, part, 6).start()
+            if pc == 0:
+                for part in range(len(PARTS)):
+                    for i in (2, 3):
+                        ag_copy(1, part, i).start()
+        prepare(n, par, 1)
         carry = [cc_src[kind] for kind in range(3)]
         for k in range(1, nz):
             cc_copy(par, k).wait_recv()
@@ -393,16 +469,6 @@
             cb_copy(par, k).wait_send()
         for k in range(1, nz):
             cc_copy(par, k).wait_send()
-
-        @pl.when(r < nr - 1)
-        def _():
-            halo_copy(par, 0).wait_send()
-            halo_copy(par, 1).wait_recv()
-
-        @pl.when(r > 0)
-        def _():
-            halo_copy(par, 1).wait_send()
-            halo_copy(par, 0).wait_recv()
 
         for kind in range(3):
             own[4 * kind : 4 * kind + 4] = carry[kind]
@@ -442,38 +508,37 @@
                 )
             cols = [jnp.concatenate(parts, axis=0) for parts in cols]
             hi, lo = split2(jnp.concatenate(cols, axis=1))
-            field[p] = dot(f_hi[...], hi) + (dot(f_hi[...], lo) + dot(f_lo[...], hi))
-        first = n == 0
+            wide = dot(f_both[...], hi)
+            field[pc, p] = wide[:chans] + (wide[chans:] + dot(f_both[:chans], lo))
+        factor = jnp.where(n == 0, 2.0, 1.0).astype(F32)
+        lanes = slice(base, base + 2 * LANES)
         for c0 in range(0, chans, ROWS_STEP):
             rows = slice(c0, c0 + ROWS_STEP)
-            lanes = slice(base, base + 2 * LANES)
+            al = alpha[rows, lanes] * factor
+            be = beta[rows, lanes] * factor
             ob = orb[rows, lanes]
-            v, w = [], []
+            f0 = field[pc, 0, rows]
+            f1 = field[pc, 1, rows]
+            new = (
+                known[0, rows, lanes] + (al * f1 - be * f0),
+                known[1, rows, lanes] - (al * f0 + be * f1),
+            )
             for p in range(2):
-                x = vbuf[par, p, rows, pl.ds(base, 4 * LANES)]
-                left = pltpu.roll(x, 1, 1)[:, LANES : 3 * LANES]
-                right = pltpu.roll(x, 4 * LANES - 1, 1)[:, LANES : 3 * LANES]
-                v.append(x[:, LANES : 3 * LANES])
-                w.append(field[p, rows, :] * ob - 0.25 * (left + right))
-            dg = diag[rows, lanes]
-            r0 = jnp.where(first, v[0] + (w[1] + dg * v[1]), rhs[0, rows, lanes])
-            r1 = jnp.where(first, v[1] - (w[0] + dg * v[0]), rhs[1, rows, lanes])
-            rhs[0, rows, lanes] = r0
-            rhs[1, rows, lanes] = r1
-            n0 = r0 + w[1]
-            n1 = r1 - w[0]
-            sc = scl[rows, lanes]
-            vbuf[1 - par, 0, rows, pl.ds(LANES + base, 2 * LANES)] = (n0 + dg * n1) * sc
-            vbuf[1 - par, 1, rows, pl.ds(LANES + base, 2 * LANES)] = (n1 - dg * n0) * sc
+                vbuf[1 - par, p, rows, pl.ds(LANES + base, 2 * LANES)] = new[p]
+                hi, lo = split2(new[p] * ob)
+                w_hi[p, rows] = hi
+                w_lo[p, rows] = lo
 
     spread_orbitals()
     load.wait()
-    densities(0, 0)
+    weigh(0, 0)
+    densities(0)
     pl.semaphore_wait(barrier, 4 + (ng - 1) + (ny - 1))
     send_far(0)
-    densities(0, 1)
+    send_direct(0)
+    weigh(0, 1)
+    densities(1)
     send_far(1)
-    send_direct()
     power_tables()
     totals(0)
     diagonal_tables()
@@ -488,14 +553,16 @@
 
     def sweep(n, c):
         par = lax.rem(n, 2)
-        carry = communicate(par)
+        carry = communicate(n, par)
         for pc in range(2):
             advance(n, par, pc, carry)
 
             @pl.when(n < SWEEPS - 1)
             def _():
-                densities(1 - par, pc)
+                densities(pc)
                 send_far(pc)
+                if pc == 0:
+                    send_direct(0)
 
             @pl.when(n == SWEEPS - 1)
             def _():
@@ -503,7 +570,6 @@
 
         @pl.when(n < SWEEPS - 1)
         def _():
-            send_direct()
             totals(1 - par)
 
         return c
@@ -528,13 +594,16 @@
         pltpu.VMEM((chans, width), F32),
         pltpu.VMEM((chans, width), F32),
         pltpu.VMEM((chans, width), F32),
-        pltpu.VMEM((2, chans, 2 * LANES), F32),
+        pltpu.VMEM((2, chans, width), F32),
+        pltpu.VMEM((chans, width), F32),
+        pltpu.VMEM((chans, width), F32),
+        pltpu.VMEM((2, 2, chans, 2 * LANES), F32),
+        pltpu.VMEM((2, chans, 2 * LANES), BF16),
+        pltpu.VMEM((2, chans, 2 * LANES), BF16),
         pltpu.VMEM((4, 2, half, LANES), F32),
         pltpu.VMEM((4, 2, half, LANES), F32),
-        pltpu.VMEM((rows, chans), BF16),
-        pltpu.VMEM((rows, chans), BF16),
-        pltpu.VMEM((chans, rows), BF16),
-        pltpu.VMEM((chans, rows), BF16),
+        pltpu.VMEM((2 * rows, chans), BF16),
+        pltpu.VMEM((2 * chans, rows), BF16),
         pltpu.VMEM((2, 8, half, LANES), F32),
         pltpu.VMEM((2, 8, half, LANES), F32),
         pltpu.VMEM((2, 7, half, LANES), F32),
@@ -569,7 +638,7 @@
         out_specs=hbm,
         scratch_shapes=scratch,
         compiler_params=pltpu.CompilerParams(
-            collective_id=0, has_side_effects=True, vmem_limit_bytes=48 << 20
+            collective_id=0, has_side_effects=True, vmem_limit_bytes=62 << 20
         ),
         name="cn_step",
     )(

time: 96.7 us -> 93.4 us (0.966)
  local copies, waits for them, and re-layouts: 5.48 us -> 2.26 us
    unnamed x15 -> x1, local copies, waits for them, and re-layouts: 5.48 us -> 2.26 us
where the time goes in v1:
time: 93.4 us; the launch traced here: 92.4 us
  Pallas kernels  90.1 us (96%)
  local copies, waits for them, and re-layouts  2.26 us (2%)
    pallas_call x1, Pallas kernels, body(): pl.pallas_call(functools.partial(kernel, (nz, nr, ng, chans, width, half)...  90.1 us
    unnamed x1, local copies, waits for them, and re-layouts  2.26 us

profile of v1, /device:TPU:32, one launch (start us, length us, event | category | flops | bytes accessed | tf_op | source)
XLA Modules:
  0.0 92.4 jit_solution(16331294264240181140)
XLA Ops:
  0.0 90.1 %cn_step.1 = f32[2,256,512]{2,1,0:T(8,128)} custom-call(f32[2,256,512]{2,1,0:T(8,128)} %wave_hbm.1, f32[9,512]{1,0:T(8,128)} %orbitals_ref.1, s32[1,256]{1,0:T(1,128)} %bitcast.5, s32[1,256]{1,0:T(1,128)} %bitcast.6, s32[1,144]{1,0:T(1,128)} %bitcast.7, f32[144,256]{1,0:T(8,128)} %density_ref.1, f32[144,256]{1,0:T(8,128)} %bitcast.4), custom_call_target="tpu_custom_call" | custom-call | tf_op jit(solution)/shard_map/cn_step/pallas_call | solution.py:634
  90.1 2.3 %copy.9 = f32[2,256,512]{2,1,0:T(8,128)} copy(f32[2,256,512]{2,1,0:T(8,128)} %cn_step.1) | data formatting | bytes 2097152

commit v2 on v1

--- a/solution.py
+++ b/solution.py
@@ -44,13 +44,19 @@
 def kernel(
     sizes,
     wave_hbm,
+    orbitals_hbm,
+    which_hbm,
+    ell_hbm,
+    order_hbm,
+    density_hbm,
+    coupling_hbm,
+    out_hbm,
     orbitals_ref,
     which_ref,
     ell_ref,
     order_ref,
     density_ref,
     coupling_ref,
-    out_hbm,
     vbuf,
     rhs,
     orb,
@@ -116,17 +122,6 @@
     def ydev(k):
         return (z, lax.rem(y + k, ny) * ng + g)
 
-    load = pltpu.make_async_copy(
-        wave_hbm, vbuf.at[0, :, :, pl.ds(LANES, width)], io_sem.at[0]
-    )
-    load.start()
-
-    zeros_edge = jnp.zeros((chans, LANES), F32)
-    for par in range(2):
-        for p in range(2):
-            vbuf[par, p, :, 0:LANES] = zeros_edge
-            vbuf[par, p, :, LANES + width : 2 * LANES + width] = zeros_edge
-
     barrier = pltpu.get_barrier_semaphore()
 
     def greet(device):
@@ -138,12 +133,44 @@
         greet(gdev(k))
     for k in range(1, ny):
         greet(ydev(k))
+    greet((z, lax.rem(r + 1, nr)))
+    greet((z, lax.rem(r + nr - 1, nr)))
+
+    loads = [
+        pltpu.make_async_copy(src, dst, io_sem.at[i])
+        for i, (src, dst) in enumerate(
+            (
+                (which_hbm, which_ref),
+                (orbitals_hbm, orbitals_ref),
+                (wave_hbm, vbuf.at[0, :, :, pl.ds(LANES, width)]),
+                (density_hbm, density_ref),
+                (order_hbm, order_ref),
+                (ell_hbm, ell_ref),
+                (coupling_hbm, coupling_ref),
+            )
+        )
+    ]
+    for load in loads:
+        load.start()
+
+    @pl.when(r == 0)
+    def _():
+        for par in range(2):
+            for p in range(2):
+                vbuf[par, p, :, 0:LANES] = jnp.zeros((chans, LANES), F32)
+
+    @pl.when(r == nr - 1)
+    def _():
+        for par in range(2):
+            for p in range(2):
+                vbuf[par, p, :, LANES + width :] = jnp.zeros((chans, LANES), F32)
 
     tiles = width // LANES
     i0 = lax.broadcasted_iota(jnp.int32, (LANES, LANES), 0)
     i1 = lax.broadcasted_iota(jnp.int32, (LANES, LANES), 1)
     tri_in = jnp.where(i0 <= i1, 1.0, 0.0).astype(BF16)
     tri_out = jnp.where(i0 > i1, 1.0, 0.0).astype(BF16)
+    lane4 = lax.broadcasted_iota(jnp.int32, (4, LANES), 1)
     lane_id = lax.broadcasted_iota(jnp.int32, (half, LANES), 1)
 
     def spread_orbitals():
@@ -157,6 +184,8 @@
                 for o in range(orbitals_ref.shape[0]):
                     value = jnp.where(pick == float(o), orbitals_ref[o : o + 1, lanes], value)
                 orb[rows, lanes] = value
+
+    def split_density():
         hi, lo = split2(density_ref[...])
         d_both[: 2 * half] = hi
         d_both[2 * half :] = lo
@@ -332,7 +361,7 @@
             for i in (3, 4):
                 rs_copy(pc, part, i).start()
 
-    def totals(par):
+    def totals():
         acc = jnp.zeros((half, LANES), F32)
         for p in range(2):
             for mh in range(2):
@@ -349,8 +378,18 @@
         own[...] = jnp.transpose(full)[0:16]
         ca_src[0] = own[0:4]
         ca_src[1] = own[4:8]
+
+    def send_totals(par):
         for k in range(1, ng):
             ca_copy(par, k).start()
+
+        @pl.when(r < nr - 1)
+        def _():
+            halo_copy(par, 0).start()
+
+        @pl.when(r > 0)
+        def _():
+            halo_copy(par, 1).start()
 
     def communicate(n, par):
         for pc in range(2):
@@ -385,14 +424,6 @@
         for k in range(1, ny):
             cb_copy(par, k).start()
 
-        @pl.when(r < nr - 1)
-        def _():
-            halo_copy(par, 0).start()
-
-        @pl.when(r > 0)
-        def _():
-            halo_copy(par, 1).start()
-
         quarter = lax.rem(lax.div(z, 2), 2)
         for pc in range(2):
             tile = 2 * pc + lax.rem(z, 2)
@@ -426,9 +457,9 @@
             peer = lax.rem(y - k + ny, ny)
             below = below + cb_buf[par, k - 1, 0] * jnp.where(peer < y, 1.0, 0.0).astype(F32)
             above = above + cb_buf[par, k - 1, 1] * jnp.where(peer > y, 1.0, 0.0).astype(F32)
-        cc_src[0] = below
-        cc_src[1] = above + own[8:12]
-        cc_src[2] = above
+        far = own[8:12]
+        cc_src[0] = jnp.where(lane4 < half, below, pltpu.roll(far, half, 1))
+        cc_src[1] = jnp.where(lane4 < half, above, pltpu.roll(far, 2 * half - LANES, 1))
         for k in range(1, nz):
             cc_copy(par, k).start()
 
@@ -455,10 +486,10 @@
                     for i in (2, 3):
                         ag_copy(1, part, i).start()
         prepare(n, par, 1)
-        carry = [cc_src[kind] for kind in range(3)]
+        carry = [cc_src[kind] for kind in range(2)]
         for k in range(1, nz):
             cc_copy(par, k).wait_recv()
-            carry = [carry[kind] + cc_buf[par, k - 1, kind] for kind in range(3)]
+            carry = [carry[kind] + cc_buf[par, k - 1, kind] for kind in range(2)]
         for pc in range(2):
             for part in range(len(PARTS)):
                 for i in range(7):
@@ -470,8 +501,12 @@
         for k in range(1, nz):
             cc_copy(par, k).wait_send()
 
-        for kind in range(3):
-            own[4 * kind : 4 * kind + 4] = carry[kind]
+        first = pltpu.roll(carry[0], LANES - half, 1)
+        second = pltpu.roll(carry[1], 2 * LANES - 2 * half, 1)
+        far = jnp.where(lane4 < LANES - half, first, second)
+        own[0:4] = carry[0]
+        own[4:8] = carry[1] + far
+        own[8:12] = carry[1]
         pad = jnp.zeros((LANES - 16, LANES), F32)
         return jnp.transpose(jnp.concatenate([own[...], pad], axis=0))[:half]
 
@@ -480,8 +515,6 @@
         for part in range(len(PARTS)):
             for i in (2, 3, 4, 5, 6):
                 ag_copy(pc, part, i).wait_recv()
-            for i in range(7):
-                ag_copy(pc, part, i).wait_send()
         for p in range(2):
             cols = [[], []]
             for mh in range(2):
@@ -529,18 +562,26 @@
                 w_hi[p, rows] = hi
                 w_lo[p, rows] = lo
 
+    loads[0].wait()
+    loads[1].wait()
     spread_orbitals()
-    load.wait()
+    loads[2].wait()
     weigh(0, 0)
+    loads[3].wait()
+    split_density()
     densities(0)
-    pl.semaphore_wait(barrier, 4 + (ng - 1) + (ny - 1))
+    pl.semaphore_wait(barrier, 4 + (ng - 1) + (ny - 1) + 2)
     send_far(0)
     send_direct(0)
     weigh(0, 1)
     densities(1)
     send_far(1)
+    loads[4].wait()
     power_tables()
-    totals(0)
+    totals()
+    send_totals(0)
+    loads[5].wait()
+    loads[6].wait()
     diagonal_tables()
 
     def store(pc):
@@ -560,6 +601,13 @@
             @pl.when(n < SWEEPS - 1)
             def _():
                 densities(pc)
+
+            for part in range(len(PARTS)):
+                for i in range(7):
+                    ag_copy(pc, part, i).wait_send()
+
+            @pl.when(n < SWEEPS - 1)
+            def _():
                 send_far(pc)
                 if pc == 0:
                     send_direct(0)
@@ -570,7 +618,8 @@
 
         @pl.when(n < SWEEPS - 1)
         def _():
-            totals(1 - par)
+            totals()
+            send_totals(1 - par)
 
         return c
 
@@ -585,10 +634,15 @@
     half = rows // 2
     ng = 8 if nr % 8 == 0 else 2
     ny = nr // ng
-    vmem = pl.BlockSpec(memory_space=pltpu.VMEM)
     hbm = pl.BlockSpec(memory_space=pl.ANY)
     dma = pltpu.SemaphoreType.DMA
     scratch = [
+        pltpu.VMEM(orbitals.shape, F32),
+        pltpu.VMEM((1, chans), jnp.int32),
+        pltpu.VMEM((1, chans), jnp.int32),
+        pltpu.VMEM((1, rows), jnp.int32),
+        pltpu.VMEM((rows, chans), F32),
+        pltpu.VMEM((rows, chans), F32),
         pltpu.VMEM((2, 2, chans, width + 2 * LANES), F32),
         pltpu.VMEM((2, chans, width), F32),
         pltpu.VMEM((chans, width), F32),
@@ -615,9 +669,9 @@
         pltpu.VMEM((2, ng - 1, 2, 4, LANES), F32),
         pltpu.VMEM((2, 4, LANES), F32),
         pltpu.VMEM((2, ny - 1, 2, 4, LANES), F32),
-        pltpu.VMEM((3, 4, LANES), F32),
-        pltpu.VMEM((2, nz - 1, 3, 4, LANES), F32),
-        dma((2,)),
+        pltpu.VMEM((2, 4, LANES), F32),
+        pltpu.VMEM((2, nz - 1, 2, 4, LANES), F32),
+        dma((7,)),
         dma((2, len(PARTS), 7)),
         dma((2, len(PARTS), 7)),
         dma((2, len(PARTS), 7)),
@@ -634,7 +688,7 @@
     return pl.pallas_call(
         functools.partial(kernel, (nz, nr, ng, chans, width, half)),
         out_shape=jax.ShapeDtypeStruct(wavefunc.shape, F32),
-        in_specs=[hbm] + [vmem] * 6,
+        in_specs=[hbm] * 7,
         out_specs=hbm,
         scratch_shapes=scratch,
         compiler_params=pltpu.CompilerParams(

time: 93.4 us -> 90.3 us (0.967); the launches traced: 92.4 us -> 90.2 us
  Pallas kernels: 90.1 us -> 87.9 us
    pallas_call x1, Pallas kernels: 90.1 us -> 87.9 us  [body(): pl.pallas_call(functools.partial(kernel, (nz, nr, ng, chans, width, half)...]
where the time goes in v2:
time: 90.3 us; the launch traced here: 90.2 us
  Pallas kernels  87.9 us (97%)
  local copies, waits for them, and re-layouts  2.26 us (3%)
    pallas_call x1, Pallas kernels, body(): pl.pallas_call(functools.partial(kernel, (nz, nr, ng, chans, width, half)...  87.9 us
    unnamed x1, local copies, waits for them, and re-layouts  2.26 us

profile of v2, /device:TPU:32, one launch (start us, length us, event | category | flops | bytes accessed | tf_op | source)
XLA Modules:
  0.0 90.2 jit_solution(12654999037116345616)
XLA Ops:
  0.0 87.9 %cn_step.1 = f32[2,256,512]{2,1,0:T(8,128)} custom-call(f32[2,256,512]{2,1,0:T(8,128)} %wave_hbm.1, f32[9,512]{1,0:T(8,128)} %orbitals_hbm.1, s32[1,256]{1,0:T(1,128)} %bitcast.5, s32[1,256]{1,0:T(1,128)} %bitcast.6, s32[1,144]{1,0:T(1,128)} %bitcast.7, f32[144,256]{1,0:T(8,128)} %density_hbm.1, f32[144,256]{1,0:T(8,128)} %bitcast.4), custom_call_target="tpu_custom_call" | custom-call | tf_op jit(solution)/shard_map/cn_step/pallas_call | solution.py:688
  87.9 2.3 %copy.9 = f32[2,256,512]{2,1,0:T(8,128)} copy(f32[2,256,512]{2,1,0:T(8,128)} %cn_step.1) | data formatting | bytes 2097152

commit v3 on v2

--- a/solution.py
+++ b/solution.py
@@ -166,10 +166,11 @@
                 vbuf[par, p, :, LANES + width :] = jnp.zeros((chans, LANES), F32)
 
     tiles = width // LANES
-    i0 = lax.broadcasted_iota(jnp.int32, (LANES, LANES), 0)
-    i1 = lax.broadcasted_iota(jnp.int32, (LANES, LANES), 1)
-    tri_in = jnp.where(i0 <= i1, 1.0, 0.0).astype(BF16)
-    tri_out = jnp.where(i0 > i1, 1.0, 0.0).astype(BF16)
+    i0 = lax.broadcasted_iota(jnp.int32, (2 * LANES, 2 * LANES), 0)
+    i1 = lax.broadcasted_iota(jnp.int32, (2 * LANES, 2 * LANES), 1)
+    inner = (i0 < LANES) & (i1 < LANES) & (i0 <= i1)
+    outer = (i0 >= LANES) & (i1 >= LANES) & (i0 > i1)
+    tri = jnp.where(inner | outer, 1.0, 0.0).astype(BF16)
     lane4 = lax.broadcasted_iota(jnp.int32, (4, LANES), 1)
     lane_id = lax.broadcasted_iota(jnp.int32, (half, LANES), 1)
 
@@ -439,13 +440,11 @@
                 up = up_t[tile, quarter, rows]
                 dn = dn_t[tile, quarter, rows]
 
-                def local(x, tri):
-                    hi = x.astype(BF16).astype(F32)
-                    both = jnp.concatenate([hi, x - hi], axis=0).astype(BF16)
-                    s = dot(both, tri)
-                    return s[:size] + s[size:]
-
-                pot[pc, z, rows] = dn * local(acc * up, tri_in) + up * local(acc * dn, tri_out)
+                pair = jnp.concatenate([acc * up, acc * dn], axis=1)
+                hi = pair.astype(BF16).astype(F32)
+                sums = dot(jnp.concatenate([hi, pair - hi], axis=0).astype(BF16), tri)
+                sums = sums[:size] + sums[size:]
+                pot[pc, z, rows] = dn * sums[:, :LANES] + up * sums[:, LANES:]
                 for i in (0, 1):
                     ag_copy(pc, part, i).start()
             if pc == 0:
@@ -692,17 +691,22 @@
         out_specs=hbm,
         scratch_shapes=scratch,
         compiler_params=pltpu.CompilerParams(
-            collective_id=0, has_side_effects=True, vmem_limit_bytes=62 << 20
+            collective_id=0, has_side_effects=True, vmem_limit_bytes=48 << 20
         ),
         name="cn_step",
     )(
-        wavefunc,
-        orbitals,
-        channel_orbital.reshape(1, chans),
-        channel_l.reshape(1, chans),
-        row_order.reshape(1, rows),
-        density,
-        coupling.T,
+        *(
+            pltpu.with_memory_space_constraint(x, pltpu.HBM)
+            for x in (
+                wavefunc,
+                orbitals,
+                channel_orbital.reshape(1, chans),
+                channel_l.reshape(1, chans),
+                row_order.reshape(1, rows),
+                density,
+                coupling.T,
+            )
+        )
     )
 
 

time: 90.3 us -> 87.9 us (0.973)
  local copies, waits for them, and re-layouts: 2.26 us -> 0.97 us
  Pallas kernels: 87.9 us -> 86.9 us
    unnamed x1, local copies, waits for them, and re-layouts: 2.26 us -> 0.97 us
    pallas_call x1, Pallas kernels: 87.9 us -> 86.9 us  [body(): pl.pallas_call(functools.partial(kernel, (nz, nr, ng, chans, width, half)...]
where the time goes in v3:
time: 87.9 us; the launch traced here: 87.8 us
  Pallas kernels  86.9 us (99%)
  local copies, waits for them, and re-layouts  0.97 us (1%)
    pallas_call x1, Pallas kernels, body(): pl.pallas_call(functools.partial(kernel, (nz, nr, ng, chans, width, half)...  86.9 us

profile of v3, /device:TPU:32, one launch (start us, length us, event | category | flops | bytes accessed | tf_op | source)
XLA Modules:
  0.0 87.8 jit_solution(14124470112744334731)
XLA Ops:
  0.0 86.9 %cn_step.1 = f32[2,256,512]{2,1,0:T(8,128)S(1)} custom-call(f32[2,256,512]{2,1,0:T(8,128)} %wave_hbm.1, f32[9,512]{1,0:T(8,128)} %orbitals_hbm.1, s32[1,256]{1,0:T(1,128)} %bitcast.5, s32[1,256]{1,0:T(1,128)} %bitcast.6, s32[1,144]{1,0:T(1,128)} %bitcast.7, f32[144,256]{1,0:T(8,128)} %density_hbm.1, f32[144,256]{1,0:T(8,128)} %bitcast.4), custom_call_target="tpu_custom_call" | custom-call | tf_op jit(solution)/shard_map/cn_step/pallas_call | solution.py:687
  86.9 1.0 %copy.9 = f32[2,256,512]{2,1,0:T(8,128)} copy(f32[2,256,512]{2,1,0:T(8,128)S(1)} %cn_step.1) | data formatting | bytes 2097152

commit v4 on v3

--- a/solution.py
+++ b/solution.py
@@ -17,6 +17,9 @@
 RS_PLAN = ((-4, -2), (-3, -1), (3, 1), (-1, -1), (1, 1), (-2, -2), (2, 2))
 AG_PLAN = ((0, 2), (0, -2), (0, 1), (0, -1), (-2, 2), (-2, 1), (2, -1))
 PARTS = ((0, 40), (40, 32))
+WHOLE = (0, 72)
+RS_WHOLE = (3, 4)
+AG_WHOLE = (2, 3)
 ROWS_STEP = 32
 
 
@@ -236,7 +239,7 @@
 
     def rs_copy(pc, part, i):
         chunk, target = RS_PLAN[i]
-        rows = pl.ds(*PARTS[part])
+        rows = pl.ds(*(WHOLE if i in RS_WHOLE else PARTS[part]))
         return pltpu.make_async_remote_copy(
             src_ref=rho.at[pc, near(chunk), rows],
             dst_ref=rsbuf.at[pc, i, rows],
@@ -248,7 +251,8 @@
 
     def ag_copy(pc, part, i):
         chunk, target = AG_PLAN[i]
-        place = pot.at[pc, near(chunk), pl.ds(*PARTS[part])]
+        rows = pl.ds(*(WHOLE if i in AG_WHOLE else PARTS[part]))
+        place = pot.at[pc, near(chunk), rows]
         return pltpu.make_async_remote_copy(
             src_ref=place,
             dst_ref=place,
@@ -358,9 +362,8 @@
                 rs_copy(pc, part, i).start()
 
     def send_direct(pc):
-        for part in range(len(PARTS)):
-            for i in (3, 4):
-                rs_copy(pc, part, i).start()
+        for i in RS_WHOLE:
+            rs_copy(pc, 0, i).start()
 
     def totals():
         acc = jnp.zeros((half, LANES), F32)
@@ -431,7 +434,7 @@
             for part in range(len(PARTS)):
                 size = PARTS[part][1]
                 rows = pl.ds(*PARTS[part])
-                for i in (3, 4, 5, 6):
+                for i in (5, 6) if part else (3, 4, 5, 6):
                     rs_copy(pc, part, i).wait_recv()
                 acc = (rho[pc, z, rows] + rsbuf[pc, 3, rows]) + (
                     rsbuf[pc, 4, rows] + rsbuf[pc, 5, rows]
@@ -448,9 +451,8 @@
                 for i in (0, 1):
                     ag_copy(pc, part, i).start()
             if pc == 0:
-                for part in range(len(PARTS)):
-                    for i in (2, 3):
-                        ag_copy(pc, part, i).start()
+                for i in AG_WHOLE:
+                    ag_copy(pc, 0, i).start()
         for k in range(1, ny):
             cb_copy(par, k).wait_recv()
             peer = lax.rem(y - k + ny, ny)
@@ -481,9 +483,8 @@
                 ag_copy(pc, part, 1).wait_recv()
                 ag_copy(pc, part, 6).start()
             if pc == 0:
-                for part in range(len(PARTS)):
-                    for i in (2, 3):
-                        ag_copy(1, part, i).start()
+                for i in AG_WHOLE:
+                    ag_copy(1, 0, i).start()
         prepare(n, par, 1)
         carry = [cc_src[kind] for kind in range(2)]
         for k in range(1, nz):
@@ -492,7 +493,8 @@
         for pc in range(2):
             for part in range(len(PARTS)):
                 for i in range(7):
-                    rs_copy(pc, part, i).wait_send()
+                    if part == 0 or i not in RS_WHOLE:
+                        rs_copy(pc, part, i).wait_send()
         for k in range(1, ng):
             ca_copy(par, k).wait_send()
         for k in range(1, ny):
@@ -512,7 +514,7 @@
     def advance(n, par, pc, carry):
         base = pc * 2 * LANES
         for part in range(len(PARTS)):
-            for i in (2, 3, 4, 5, 6):
+            for i in (4, 5, 6) if part else (2, 3, 4, 5, 6):
                 ag_copy(pc, part, i).wait_recv()
         for p in range(2):
             cols = [[], []]
@@ -603,7 +605,8 @@
 
             for part in range(len(PARTS)):
                 for i in range(7):
-                    ag_copy(pc, part, i).wait_send()
+                    if part == 0 or i not in AG_WHOLE:
+                        ag_copy(pc, part, i).wait_send()
 
             @pl.when(n < SWEEPS - 1)
             def _():

time: 87.9 us -> 87.8 us (level)
  no operation moved by 1% of the time
where the time goes in v4:
time: 87.8 us
  Pallas kernels  86.8 us (99%)
  local copies, waits for them, and re-layouts  0.97 us (1%)
    pallas_call x1, Pallas kernels, body(): pl.pallas_call(functools.partial(kernel, (nz, nr, ng, chans, width, half)...  86.8 us

profile of v4, /device:TPU:32, one launch (start us, length us, event | category | flops | bytes accessed | tf_op | source)
XLA Modules:
  0.0 87.8 jit_solution(6363915286794504275)
XLA Ops:
  0.0 86.8 %cn_step.1 = f32[2,256,512]{2,1,0:T(8,128)S(1)} custom-call(f32[2,256,512]{2,1,0:T(8,128)} %wave_hbm.1, f32[9,512]{1,0:T(8,128)} %orbitals_hbm.1, s32[1,256]{1,0:T(1,128)} %bitcast.5, s32[1,256]{1,0:T(1,128)} %bitcast.6, s32[1,144]{1,0:T(1,128)} %bitcast.7, f32[144,256]{1,0:T(8,128)} %density_hbm.1, f32[144,256]{1,0:T(8,128)} %bitcast.4), custom_call_target="tpu_custom_call" | custom-call | tf_op jit(solution)/shard_map/cn_step/pallas_call | solution.py:690
  86.8 1.0 %copy.9 = f32[2,256,512]{2,1,0:T(8,128)} copy(f32[2,256,512]{2,1,0:T(8,128)S(1)} %cn_step.1) | data formatting | bytes 2097152

commit v5 on v4

--- a/solution.py
+++ b/solution.py
@@ -358,7 +358,7 @@
 
     def send_far(pc):
         for part in range(len(PARTS)):
-            for i in (0, 1, 2):
+            for i in (0, 2, 1):
                 rs_copy(pc, part, i).start()
 
     def send_direct(pc):

time: 87.8 us -> 87.9 us (level)
  no operation moved by 1% of the time
where the time goes in v5:
time: 87.9 us; the launch traced here: 87.8 us
  Pallas kernels  86.8 us (99%)
  local copies, waits for them, and re-layouts  0.97 us (1%)
    pallas_call x1, Pallas kernels, body(): pl.pallas_call(functools.partial(kernel, (nz, nr, ng, chans, width, half)...  86.8 us

profile of v5, /device:TPU:32, one launch (start us, length us, event | category | flops | bytes accessed | tf_op | source)
XLA Modules:
  0.0 87.8 jit_solution(12041405409473650441)
XLA Ops:
  0.0 86.8 %cn_step.1 = f32[2,256,512]{2,1,0:T(8,128)S(1)} custom-call(f32[2,256,512]{2,1,0:T(8,128)} %wave_hbm.1, f32[9,512]{1,0:T(8,128)} %orbitals_hbm.1, s32[1,256]{1,0:T(1,128)} %bitcast.5, s32[1,256]{1,0:T(1,128)} %bitcast.6, s32[1,144]{1,0:T(1,128)} %bitcast.7, f32[144,256]{1,0:T(8,128)} %density_hbm.1, f32[144,256]{1,0:T(8,128)} %bitcast.4), custom_call_target="tpu_custom_call" | custom-call | tf_op jit(solution)/shard_map/cn_step/pallas_call | solution.py:690
  86.8 1.0 %copy.9 = f32[2,256,512]{2,1,0:T(8,128)} copy(f32[2,256,512]{2,1,0:T(8,128)S(1)} %cn_step.1) | data formatting | bytes 2097152
